TPU v7x, 32 devices: a whole 2x2x4 slice. The times are simulated.
32 devices in a mesh: tile: 16 (over z, x, core), agent: 2 (over y).
Axes of the slice: x: 2, y: 2, z: 4, core: 2. Of those that a mesh axis runs over, the one named last changes fastest.
Arguments:
- states: float32 [2, 8, 32, 256], P('agent', None, 'tile'), may hold values from -6 to 6
- footprints: float32 [16, 16, 64, 512], P('agent', 'tile'), may hold values from -0.25 to 0.25
- offsets: int32 [16, 16], P('agent', 'tile'), may hold values from 0 to 1984, as said below
- measured: float32 [16, 8, 2048], P('agent', None, 'tile'), may hold values from -9 to 9
- weights: float32 [16, 8, 2048], P('agent', None, 'tile'), may hold values from 0.2 to 5
Outputs:
- new_states: float32 [2, 8, 32, 256], P('agent', None, 'tile')
- prior_volume: float32 [8, 32, 256], P(None, 'tile')
Inputs may be any that keep to these rules, and one draw needn't show every extreme that they name: For one agent and one tile t, the values offsets[v, t] // 128 differ between the agent's 8 views v.
All inputs are finite; a program needn't handle non-finite values.
Results may differ from a plain program's by a relative error of at most 0.0003.
Values sent between devices are 32-bit elements; how exact they have to be, the bound alone decides.
A program may use at most 64 MiB of HBM per device.

v0:
```python
import jax
import jax.numpy as jnp
from jax import lax
from jax.sharding import PartitionSpec as P

SWEEPS = 2


STEP_SIZE = 0.25
RELAX = 0.6
QRATIO = 0.6


def with_halo(value, sides, width):
    for axis, dim in sides:
        count, length = (lax.axis_size(axis), value.shape[dim])
        up = [(i, (i + 1) % count) for i in range(count - 1)]
        down = [(j, i) for i, j in up]
        last = lax.slice_in_dim(value, length - width, length, axis=dim)
        first = lax.slice_in_dim(value, 0, width, axis=dim)
        before = lax.ppermute(last, axis, up)
        after = lax.ppermute(first, axis, down)
        value = jnp.concatenate([before, value, after], axis=dim)
    return value


def neighbour_table():
    offsets_nb = []
    for a in (-1, 0, 1):
        for b in (-1, 0, 1):
            for c in (-1, 0, 1):
                if a != 0 or b != 0 or c != 0:
                    offsets_nb.append((a, b, c, 1.0 / (a * a + b * b + c * c) ** 0.5))
    total = sum((item[3] for item in offsets_nb))
    return [(a, b, c, 4.0 * w / total) for a, b, c, w in offsets_nb]


def sweep_update(padded, average):
    depth, height, width = average.shape
    centre = padded[1 : 1 + depth, 1 : 1 + height, 1 : 1 + width]
    numerator = average
    denominator = jnp.ones_like(average)
    for a, b, c, weight_nb in neighbour_table():
        neighbour = padded[1 + a : 1 + a + depth, 1 + b : 1 + b + height, 1 + c : 1 + c + width]
        differ = centre - neighbour
        powered = jnp.power(differ * differ, 0.4)
        coefficient = weight_nb * (1.0 + QRATIO * powered) / ((1.0 + powered) * (1.0 + powered))
        numerator = numerator + coefficient * neighbour
        denominator = denominator + coefficient
    return numerator / denominator


def shards(states, footprints, offsets, measured, weights):
    current = states[0]
    blocks = footprints[:, 0]
    offsets_dev = offsets[:, 0]
    slices, height, width = current.shape
    views, foot, pixels = blocks.shape
    share = measured.shape[2]
    n_tile = lax.axis_size("tile")
    n_agent = lax.axis_size("agent")
    zero_index = jnp.int32(0)
    pieces_count = (2 * share + foot - 2) // share
    window_width = pieces_count * share
    start_owner = offsets_dev // share
    local_start = offsets_dev - start_owner * share
    owner_ids = jnp.arange(n_tile, dtype=jnp.int32)
    piece_ids = jnp.arange(pieces_count, dtype=jnp.int32)
    selector = (
        start_owner[None, None, :] + piece_ids[None, :, None] == owner_ids[:, None, None]
    ).astype(jnp.float32)
    volume = current.reshape(slices, pixels)
    projected = jnp.einsum("sp,vbp->vsb", volume, blocks, precision=lax.Precision.HIGHEST)
    placed = jnp.stack(
        [
            lax.dynamic_update_slice(
                jnp.zeros((slices, window_width), jnp.float32),
                projected[view],
                (zero_index, local_start[view]),
            )
            for view in range(views)
        ]
    ).reshape(views, slices, pieces_count, share)
    outgoing = jnp.einsum("djv,vsjc->djsc", selector, placed, precision=lax.Precision.HIGHEST)
    incoming = lax.all_to_all(outgoing, "tile", split_axis=0, concat_axis=0, tiled=True)
    chosen = lax.all_to_all(selector, "tile", split_axis=0, concat_axis=0, tiled=True)
    share_sum = jnp.einsum("tjv,tjsc->vsc", chosen, incoming, precision=lax.Precision.HIGHEST)
    residual_share = weights * (share_sum - measured)
    returned = jnp.einsum("tjv,vsc->tjsc", chosen, residual_share, precision=lax.Precision.HIGHEST)
    backward = lax.all_to_all(returned, "tile", split_axis=0, concat_axis=0, tiled=True)
    collected = jnp.einsum("djv,djsc->vsjc", selector, backward, precision=lax.Precision.HIGHEST)
    collected = collected.reshape(views, slices, window_width)
    windows = jnp.stack(
        [
            lax.dynamic_slice(collected[view], (zero_index, local_start[view]), (slices, foot))
            for view in range(views)
        ]
    )
    gradient = jnp.einsum("vsb,vbp->sp", windows, blocks, precision=lax.Precision.HIGHEST)
    fitted = current - STEP_SIZE * gradient.reshape(slices, height, width)
    reflect = 2.0 * fitted - current
    brick_mean = lax.psum_scatter(reflect, "agent", scatter_dimension=0, tiled=True) / n_agent
    smoothed = brick_mean
    for sweep_index in range(SWEEPS):
        padded = with_halo(smoothed, (("tile", 1), ("agent", 0)), 1)
        padded = jnp.pad(padded, ((0, 0), (0, 0), (1, 1)))
        smoothed = sweep_update(padded, brick_mean)
    prior_vol = lax.all_gather(smoothed, "agent", axis=0, tiled=True)
    current = (1.0 - RELAX) * current + RELAX * (2.0 * prior_vol - reflect)
    return (current[None], prior_vol)


def solution(mesh):
    in_specs = (
        P("agent", None, "tile", None),
        P("agent", "tile", None, None),
        P("agent", "tile"),
        P("agent", None, "tile"),
        P("agent", None, "tile"),
    )
    out_specs = (P("agent", None, "tile", None), P(None, "tile", None))
    return jax.shard_map(shards, mesh=mesh, in_specs=in_specs, out_specs=out_specs, check_vma=False)
```

profile of v0, /device:TPU:0, one launch (start us, length us, event | category | flops | bytes accessed | tf_op | source)
XLA Modules:
  0.0 100.1 jit_solution(11030375158423234259)
XLA Ops:
  0.6 0.7 bitcast_subtract_fusion.1
  1.3 0.6 fusion.25
  1.9 7.4 %all-to-all-start = ((f32[16,2,8]{2,1,0:T(2,128)}), f32[16,2,8]{2,1,0:T(2,128)S(1)}, u32[]{:S(2)}, u32[]{:S(2)}) async-start(f32[16,2,8]{2,1,0:T(2,128)} %get-tuple-element.32), calls=%async_computation | async-start | bytes 32768 | tf_op jit(solution)/shard_map/all_to_all | solution.py:86
  9.3 0.7 fusion.30
  14.5 0.0 copy-start.1
  20.3 0.0 copy-done.1
  20.3 2.6 %convolution_bitcast_fusion.1 = f32[8,8,64]{2,1,0:T(8,128)S(1)} fusion(f32[8,512,1]{1,0,2:T(8,128)S(1)} %reshape.103, f32[8,1,64,512]{3,2,1,0:T(8,128)} %param.6), kind=kOutput, calls=%fused_computation.1 | convolution fusion | flops 25165824 | bytes 1081344 | tf_op jit(solution)/shard_map/sp,vbp->vsb/dot_general | solution.py:73
  23.6 0.3 dynamic_update_slice.32
  23.9 0.1 copy.19
  24.7 0.3 dynamic_update_slice.33
  25.7 0.3 dynamic_update_slice.34
  26.6 0.3 dynamic_update_slice.35
  27.6 0.3 dynamic_update_slice.36
  28.6 0.3 dynamic_update_slice.37
  29.5 0.3 dynamic_update_slice.38
  30.5 0.3 dynamic_update_slice.39
  30.8 0.0 copy-start.3
  30.9 0.3 fusion.10
  31.1 0.0 copy-start
  31.2 0.0 all-to-all-done
  31.2 13.9 %all_to_all.15 = f32[16,2,8,128]{3,2,1,0:T(8,128)S(1)} all-to-all(f32[16,2,8,128]{3,2,1,0:T(8,128)S(1)} %bitcast.99), channel_id=1, replica_groups=mesh['tile'=16,'agent'=2] {'tile'}, dimensions={0} | all-to-all | bytes 262144 | tf_op jit(solution)/shard_map/all_to_all | solution.py:85
  45.1 0.2 fusion.7
  45.3 0.2 fusion.16
  45.6 0.7 copy.26
  46.3 3.5 %all-to-all-start.2 = ((f32[16,2,8,128]{3,2,1,0:T(8,128)}), f32[16,2,8,128]{3,2,1,0:T(8,128)S(1)}, u32[]{:S(2)}, u32[]{:S(2)}) async-start(f32[16,2,8,128]{3,2,1,0:T(8,128)} %copy.26), calls=%async_computation.2 | async-start | bytes 262144 | tf_op jit(solution)/shard_map/all_to_all | solution.py:90
  49.8 0.0 copy-start.4
  49.8 0.6 copy-done.4
  50.5 0.6 dynamic-slice
  51.7 6.0 %all-to-all-done.2 = f32[16,2,8,128]{3,2,1,0:T(8,128)S(1)} async-done(((f32[16,2,8,128]{3,2,1,0:T(8,128)}), f32[16,2,8,128]{3,2,1,0:T(8,128)S(1)}, u32[]{:S(2)}, u32[]{:S(2)}) %all-to-all-start.2) | async-done | bytes 131104 | tf_op jit(solution)/shard_map/all_to_all | solution.py:90
  57.7 0.2 convolution_bitcast_fusion
  57.9 0.1 constant_dynamic-update-slice_fusion.15
  58.0 0.1 constant_dynamic-update-slice_fusion.14
  58.1 0.1 constant_dynamic-update-slice_fusion.13
  58.2 0.1 constant_dynamic-update-slice_fusion.12
  58.2 0.1 constant_dynamic-update-slice_fusion.11
  58.3 0.1 constant_dynamic-update-slice_fusion.10
  58.4 0.1 constant_dynamic-update-slice_fusion.9
  58.5 0.1 constant_dynamic-update-slice_fusion.8
  58.5 0.0 copy-done
  58.5 0.6 fusion.3
  59.2 8.1 %all-reduce.2 = f32[8,2,256]{2,0,1:T(8,128)S(1)} all-reduce(f32[8,2,256]{2,0,1:T(8,128)S(1)} %fusion.3), channel_id=2, replica_groups=mesh['tile'=16,'agent'=2] {'agent'}, use_global_device_ids=true, to_apply=%region_0.1.clone | all-reduce | flops 4096 | bytes 32768
  67.3 1.3 %collective-permute-start = (f32[4,1,256]{2,0,1:T(4,128)S(1)}, f32[4,1,256]{2,0,1:T(4,128)S(1)}, u32[]{:S(2)}, u32[]{:S(2)}) collective-permute-start(f32[4,1,256]{2,0,1:T(4,128)S(1)} %get-tuple-element.30), channel_id=1, source_target_pairs={{0,2},{2,4},{4,6},{6,8},{8,10},{10,12},{12,14},{14,16},{16,18},{18... | collective-permute-start | bytes 12296 | tf_op jit(solution)/shard_map/ppermute | solution.py:21
  68.6 1.3 %collective-permute-start.1 = (f32[4,1,256]{2,0,1:T(4,128)S(1)}, f32[4,1,256]{2,0,1:T(4,128)S(1)}, u32[]{:S(2)}, u32[]{:S(2)}) collective-permute-start(f32[4,1,256]{2,0,1:T(4,128)S(1)} %get-tuple-element.31), channel_id=1, source_target_pairs={{2,0},{4,2},{6,4},{8,6},{10,8},{12,10},{14,12},{16,14},{18,16},{20... | collective-permute-start | bytes 12296 | tf_op jit(solution)/shard_map/ppermute | solution.py:22
  69.9 0.0 collective-permute-done
  69.9 1.7 %collective-permute-done.1 = f32[4,1,256]{2,0,1:T(4,128)S(1)} collective-permute-done((f32[4,1,256]{2,0,1:T(4,128)S(1)}, f32[4,1,256]{2,0,1:T(4,128)S(1)}, u32[]{:S(2)}, u32[]{:S(2)}) %collective-permute-start.1) | collective-permute-done | bytes 4128 | tf_op jit(solution)/shard_map/ppermute | solution.py:22
  71.7 2.5 %collective-permute-start.2 = (f32[1,4,256]{2,0,1:T(1,128)S(1)}, f32[1,4,256]{2,0,1:T(1,128)S(1)}, u32[]{:S(2)}, u32[]{:S(2)}) collective-permute-start(f32[1,4,256]{2,0,1:T(1,128)S(1)} %get-tuple-element.26), channel_id=1, source_target_pairs={{0,1},{2,3},{4,5},{6,7},{8,9},{10,11},{12,13},{14,15},{16,17},{18,... | collective-permute-start | bytes 12296 | tf_op jit(solution)/shard_map/ppermute | solution.py:21
  74.1 1.3 %collective-permute-start.3 = (f32[1,4,256]{2,0,1:T(1,128)S(1)}, f32[1,4,256]{2,0,1:T(1,128)S(1)}, u32[]{:S(2)}, u32[]{:S(2)}) collective-permute-start(f32[1,4,256]{2,0,1:T(1,128)S(1)} %get-tuple-element.27), channel_id=1, source_target_pairs={{1,0},{3,2},{5,4},{7,6},{9,8},{11,10},{13,12},{15,14},{17,16},{19,... | collective-permute-start | bytes 12296 | tf_op jit(solution)/shard_map/ppermute | solution.py:22
  75.4 0.0 collective-permute-done.2
  75.5 4.2 %collective-permute-done.3 = f32[1,4,256]{2,0,1:T(1,128)S(1)} collective-permute-done((f32[1,4,256]{2,0,1:T(1,128)S(1)}, f32[1,4,256]{2,0,1:T(1,128)S(1)}, u32[]{:S(2)}, u32[]{:S(2)}) %collective-permute-start.3) | collective-permute-done | bytes 4128 | tf_op jit(solution)/shard_map/ppermute | solution.py:22
  79.6 0.1 select_maximum_fusion.4
  79.8 0.4 add_divide_fusion.1
  80.2 2.4 %collective-permute-start.4 = (f32[4,1,256]{2,0,1:T(4,128)S(1)}, f32[4,1,256]{2,0,1:T(4,128)S(1)}, u32[]{:S(2)}, u32[]{:S(2)}) collective-permute-start(f32[4,1,256]{2,0,1:T(4,128)S(1)} %get-tuple-element.28), channel_id=1, source_target_pairs={{0,2},{2,4},{4,6},{6,8},{8,10},{10,12},{12,14},{14,16},{16,18},{18... | collective-permute-start | bytes 12296 | tf_op jit(solution)/shard_map/ppermute | solution.py:21
  82.6 1.3 %collective-permute-start.5 = (f32[4,1,256]{2,0,1:T(4,128)S(1)}, f32[4,1,256]{2,0,1:T(4,128)S(1)}, u32[]{:S(2)}, u32[]{:S(2)}) collective-permute-start(f32[4,1,256]{2,0,1:T(4,128)S(1)} %get-tuple-element.29), channel_id=1, source_target_pairs={{2,0},{4,2},{6,4},{8,6},{10,8},{12,10},{14,12},{16,14},{18,16},{20... | collective-permute-start | bytes 12296 | tf_op jit(solution)/shard_map/ppermute | solution.py:22
  83.9 0.0 collective-permute-done.4
  84.0 2.7 %collective-permute-done.5 = f32[4,1,256]{2,0,1:T(4,128)S(1)} collective-permute-done((f32[4,1,256]{2,0,1:T(4,128)S(1)}, f32[4,1,256]{2,0,1:T(4,128)S(1)}, u32[]{:S(2)}, u32[]{:S(2)}) %collective-permute-start.5) | collective-permute-done | bytes 4128 | tf_op jit(solution)/shard_map/ppermute | solution.py:22
  86.7 1.7 %collective-permute-start.6 = (f32[1,4,256]{2,0,1:T(1,128)S(1)}, f32[1,4,256]{2,0,1:T(1,128)S(1)}, u32[]{:S(2)}, u32[]{:S(2)}) collective-permute-start(f32[1,4,256]{2,0,1:T(1,128)S(1)} %get-tuple-element.24), channel_id=1, source_target_pairs={{0,1},{2,3},{4,5},{6,7},{8,9},{10,11},{12,13},{14,15},{16,17},{18,... | collective-permute-start | bytes 12296 | tf_op jit(solution)/shard_map/ppermute | solution.py:21
  88.3 1.3 %collective-permute-start.7 = (f32[1,4,256]{2,0,1:T(1,128)S(1)}, f32[1,4,256]{2,0,1:T(1,128)S(1)}, u32[]{:S(2)}, u32[]{:S(2)}) collective-permute-start(f32[1,4,256]{2,0,1:T(1,128)S(1)} %get-tuple-element.25), channel_id=1, source_target_pairs={{1,0},{3,2},{5,4},{7,6},{9,8},{11,10},{13,12},{15,14},{17,16},{19,... | collective-permute-start | bytes 12296 | tf_op jit(solution)/shard_map/ppermute | solution.py:22
  89.7 0.0 collective-permute-done.6
  89.7 4.2 %collective-permute-done.7 = f32[1,4,256]{2,0,1:T(1,128)S(1)} collective-permute-done((f32[1,4,256]{2,0,1:T(1,128)S(1)}, f32[1,4,256]{2,0,1:T(1,128)S(1)}, u32[]{:S(2)}, u32[]{:S(2)}) %collective-permute-start.7) | collective-permute-done | bytes 4128 | tf_op jit(solution)/shard_map/ppermute | solution.py:22
  93.9 0.1 select_maximum_fusion
  94.0 0.4 add_divide_fusion
  94.4 4.4 %all_gather.3 = f32[8,2,256]{2,1,0:T(2,128)S(1)} all-gather(f32[4,2,256]{2,1,0:T(2,128)S(1)} %copy.15), channel_id=1, replica_groups=mesh['tile'=16,'agent'=2] {'agent'}, dimensions={0}, use_global_device_ids=true | all-gather | bytes 24576 | tf_op jit(solution)/shard_map/all_gather | solution.py:108
  98.8 0.6 copy.17
  99.4 0.6 copy.85
  (32 shorter events, 0.2 us)
Async XLA Ops:
  1.9 29.3 %all-to-all-start = ((f32[16,2,8]{2,1,0:T(2,128)}), f32[16,2,8]{2,1,0:T(2,128)S(1)}, u32[]{:S(2)}, u32[]{:S(2)}) async-start(f32[16,2,8]{2,1,0:T(2,128)} %get-tuple-element.32), calls=%async_computation | async-start | bytes 32768 | tf_op jit(solution)/shard_map/all_to_all | solution.py:86
  14.5 5.8 %copy-start.1 = (f32[1,8,2,256]{3,2,1,0:T(2,128)S(1)}, f32[1,8,2,256]{3,2,1,0:T(2,128)}, u32[]{:S(2)}) copy-start(f32[1,8,2,256]{3,2,1,0:T(2,128)} %param.5) | copy-start | bytes 49156
  30.8 14.5 %copy-start.2 = (f32[8,8,128]{2,1,0:T(8,128)S(1)}, f32[8,8,128]{2,1,0:T(8,128)}, u32[]{:S(2)}) copy-start(f32[8,8,128]{2,1,0:T(8,128)} %param.9) | copy-start | bytes 98308
  30.8 14.5 %copy-start.3 = (f32[8,8,128]{2,1,0:T(8,128)S(1)}, f32[8,8,128]{2,1,0:T(8,128)}, u32[]{:S(2)}) copy-start(f32[8,8,128]{2,1,0:T(8,128)} %param.8) | copy-start | bytes 98308
  31.1 27.4 %copy-start = (f32[8,1,64,512]{3,2,1,0:T(8,128)S(1)}, f32[8,1,64,512]{3,2,1,0:T(8,128)}, u32[]{:S(2)}) copy-start(f32[8,1,64,512]{3,2,1,0:T(8,128)} %param.6) | copy-start | bytes 3145732
  46.3 11.4 %all-to-all-start.2 = ((f32[16,2,8,128]{3,2,1,0:T(8,128)}), f32[16,2,8,128]{3,2,1,0:T(8,128)S(1)}, u32[]{:S(2)}, u32[]{:S(2)}) async-start(f32[16,2,8,128]{3,2,1,0:T(8,128)} %copy.26), calls=%async_computation.2 | async-start | bytes 262144 | tf_op jit(solution)/shard_map/all_to_all | solution.py:90
  49.8 0.7 copy-start.4
  67.3 2.6 %collective-permute-start = (f32[4,1,256]{2,0,1:T(4,128)S(1)}, f32[4,1,256]{2,0,1:T(4,128)S(1)}, u32[]{:S(2)}, u32[]{:S(2)}) collective-permute-start(f32[4,1,256]{2,0,1:T(4,128)S(1)} %get-tuple-element.30), channel_id=1, source_target_pairs={{0,2},{2,4},{4,6},{6,8},{8,10},{10,12},{12,14},{14,16},{16,18},{18... | collective-permute-start | bytes 12296 | tf_op jit(solution)/shard_map/ppermute | solution.py:21
  68.6 3.1 %collective-permute-start.1 = (f32[4,1,256]{2,0,1:T(4,128)S(1)}, f32[4,1,256]{2,0,1:T(4,128)S(1)}, u32[]{:S(2)}, u32[]{:S(2)}) collective-permute-start(f32[4,1,256]{2,0,1:T(4,128)S(1)} %get-tuple-element.31), channel_id=1, source_target_pairs={{2,0},{4,2},{6,4},{8,6},{10,8},{12,10},{14,12},{16,14},{18,16},{20... | collective-permute-start | bytes 12296 | tf_op jit(solution)/shard_map/ppermute | solution.py:22
  71.7 3.8 %collective-permute-start.2 = (f32[1,4,256]{2,0,1:T(1,128)S(1)}, f32[1,4,256]{2,0,1:T(1,128)S(1)}, u32[]{:S(2)}, u32[]{:S(2)}) collective-permute-start(f32[1,4,256]{2,0,1:T(1,128)S(1)} %get-tuple-element.26), channel_id=1, source_target_pairs={{0,1},{2,3},{4,5},{6,7},{8,9},{10,11},{12,13},{14,15},{16,17},{18,... | collective-permute-start | bytes 12296 | tf_op jit(solution)/shard_map/ppermute | solution.py:21
  74.1 5.5 %collective-permute-start.3 = (f32[1,4,256]{2,0,1:T(1,128)S(1)}, f32[1,4,256]{2,0,1:T(1,128)S(1)}, u32[]{:S(2)}, u32[]{:S(2)}) collective-permute-start(f32[1,4,256]{2,0,1:T(1,128)S(1)} %get-tuple-element.27), channel_id=1, source_target_pairs={{1,0},{3,2},{5,4},{7,6},{9,8},{11,10},{13,12},{15,14},{17,16},{19,... | collective-permute-start | bytes 12296 | tf_op jit(solution)/shard_map/ppermute | solution.py:22
  80.2 3.8 %collective-permute-start.4 = (f32[4,1,256]{2,0,1:T(4,128)S(1)}, f32[4,1,256]{2,0,1:T(4,128)S(1)}, u32[]{:S(2)}, u32[]{:S(2)}) collective-permute-start(f32[4,1,256]{2,0,1:T(4,128)S(1)} %get-tuple-element.28), channel_id=1, source_target_pairs={{0,2},{2,4},{4,6},{6,8},{8,10},{10,12},{12,14},{14,16},{16,18},{18... | collective-permute-start | bytes 12296 | tf_op jit(solution)/shard_map/ppermute | solution.py:21
  82.6 4.0 %collective-permute-start.5 = (f32[4,1,256]{2,0,1:T(4,128)S(1)}, f32[4,1,256]{2,0,1:T(4,128)S(1)}, u32[]{:S(2)}, u32[]{:S(2)}) collective-permute-start(f32[4,1,256]{2,0,1:T(4,128)S(1)} %get-tuple-element.29), channel_id=1, source_target_pairs={{2,0},{4,2},{6,4},{8,6},{10,8},{12,10},{14,12},{16,14},{18,16},{20... | collective-permute-start | bytes 12296 | tf_op jit(solution)/shard_map/ppermute | solution.py:22
  86.7 3.0 %collective-permute-start.6 = (f32[1,4,256]{2,0,1:T(1,128)S(1)}, f32[1,4,256]{2,0,1:T(1,128)S(1)}, u32[]{:S(2)}, u32[]{:S(2)}) collective-permute-start(f32[1,4,256]{2,0,1:T(1,128)S(1)} %get-tuple-element.24), channel_id=1, source_target_pairs={{0,1},{2,3},{4,5},{6,7},{8,9},{10,11},{12,13},{14,15},{16,17},{18,... | collective-permute-start | bytes 12296 | tf_op jit(solution)/shard_map/ppermute | solution.py:21
  88.3 5.5 %collective-permute-start.7 = (f32[1,4,256]{2,0,1:T(1,128)S(1)}, f32[1,4,256]{2,0,1:T(1,128)S(1)}, u32[]{:S(2)}, u32[]{:S(2)}) collective-permute-start(f32[1,4,256]{2,0,1:T(1,128)S(1)} %get-tuple-element.25), channel_id=1, source_target_pairs={{1,0},{3,2},{5,4},{7,6},{9,8},{11,10},{13,12},{15,14},{17,16},{19,... | collective-permute-start | bytes 12296 | tf_op jit(solution)/shard_map/ppermute | solution.py:22
where the time goes:
time: 102 us; the launch traced here: 100 us
  blocking collectives  26.4 us (26%)
  starting transfers between devices  23.9 us (23%)
  waiting for transfers between devices  18.9 us (19%)
  between operations  17.2 us (17%)
  local copies, waits for them, and re-layouts  7.2 us (7%)
  matrix products  4.09 us (4%)
  other arithmetic  2.39 us (2%)
    all_to_all x1, blocking collectives, shards(): lax.all_to_all(outgoing, 'tile', split_axis=0, concat_axis=0, tiled=True)  13.9 us
    ppermute x4, waiting for transfers between devices, with_halo(): after = lax.ppermute(first, axis, down)  12.9 us
    unnamed x1, blocking collectives  8.12 us
    ppermute x4, starting transfers between devices, with_halo(): before = lax.ppermute(last, axis, up)  7.85 us
    all_to_all x1, starting transfers between devices, shards(): lax.all_to_all(selector, 'tile', split_axis=0, concat_axis=0, tiled=True)  7.36 us
    all_to_all x1, waiting for transfers between devices, shards(): lax.all_to_all(returned, 'tile', split_axis=0, concat_axis=0, tiled=True)  6 us
    ppermute x4, starting transfers between devices, with_halo(): after = lax.ppermute(first, axis, down)  5.17 us
    all_gather x1, blocking collectives, shards(): prior_vol = lax.all_gather(smoothed, 'agent', axis=0, tiled=True)  4.42 us
  transfers between devices with their start and end apart: 10, of which 5 were waited for; matrix products, arithmetic and copies ran while one was open for 7% of the time, Pallas kernels for 0%

commit v1 on v0

v1 whole, which is shorter than its diff:
```python
import functools

import jax
import jax.numpy as jnp
from jax import lax
from jax.experimental import pallas as pl
from jax.experimental.pallas import tpu as pltpu
from jax.sharding import PartitionSpec as P

SWEEPS = 2
STEP_SIZE = 0.25
RELAX = 0.6
QRATIO = 0.6
MESH = pl.DeviceIdType.MESH
EXACT = lax.Precision.HIGHEST


def neighbour_table():
    offsets_nb = []
    for a in (-1, 0, 1):
        for b in (-1, 0, 1):
            for c in (-1, 0, 1):
                if a != 0 or b != 0 or c != 0:
                    offsets_nb.append((a, b, c, a * a + b * b + c * c))
    total = sum(1.0 / item[3] ** 0.5 for item in offsets_nb)
    scale = {n: 4.0 / n**0.5 / total for n in (1, 2, 3)}
    return offsets_nb, scale


def shift_zero(value, step, dim):
    if step == 0:
        return value
    size = value.shape[dim]
    index = lax.broadcasted_iota(jnp.int32, value.shape, dim)
    rolled = pltpu.roll(value, (-step) % size, dim)
    inside = index < size - 1 if step == 1 else index >= 1
    return jnp.where(inside, rolled, 0.0)


def sweep_rows(rows, averages):
    offsets_nb, scale = neighbour_table()
    shifted = [
        {(a, c): shift_zero(shift_zero(row, a, 0), c, 1) for a in (-1, 0, 1) for c in (-1, 0, 1)}
        for row in rows
    ]
    result = []
    for r in range(1, len(rows) - 1):
        centre = rows[r]
        num, den = {}, {}
        for a, b, c, kind in offsets_nb:
            neighbour = shifted[r + b][(a, c)]
            differ = centre - neighbour
            powered = jnp.exp(0.4 * jnp.log(differ * differ))
            inverse = 1.0 / (1.0 + powered)
            coefficient = inverse * (QRATIO + (1.0 - QRATIO) * inverse)
            num[kind] = num[kind] + coefficient * neighbour if kind in num else coefficient * neighbour
            den[kind] = den[kind] + coefficient if kind in den else coefficient
        top = averages[r] + sum(scale[n] * num[n] for n in num)
        bottom = 1.0 + sum(scale[n] * den[n] for n in den)
        result.append(top / bottom)
    return result


def each(count, body, first=0):
    if count <= 16:
        for k in range(first, count):
            body(k)
    else:
        lax.fori_loop(first, count, lambda k, c: (body(k), c)[1], 0)


def kernel(
    n_tile, n_agent, states_ref, blocks_hbm, offsets_ref, measured_ref, weights_ref,
    new_ref, prior_ref,
    fp, placed, chosen, acc, fsend, frecv, bsend, brecv, rsend, rrecv,
    fp_sem, fss, frs, bss, brs, rss, rrs,
):
    me, ag = lax.axis_index("tile"), lax.axis_index("agent")
    _, slices, height, width = states_ref.shape
    views, foot, pixels = fp.shape
    share = measured_ref.shape[2]
    pieces = placed.shape[1]
    window = -(-pieces * share // 128) * 128

    blocks_copy = pltpu.make_async_copy(blocks_hbm.at[:, 0], fp, fp_sem)
    blocks_copy.start()

    barrier = pltpu.get_barrier_semaphore()

    def greet(tile, agent):
        pl.semaphore_signal(
            barrier, inc=1, device_id={"tile": tile, "agent": agent}, device_id_type=MESH
        )

    each(n_tile, lambda k: greet(lax.rem(me + k, n_tile), ag), 1)
    has_low, has_high = me > 0, me < n_tile - 1
    for k in range(1, n_agent):
        other = lax.rem(ag + k, n_agent)
        greet(me, other)

        @pl.when(has_low)
        def _():
            greet(me - 1, other)

        @pl.when(has_high)
        def _():
            greet(me + 1, other)

    start = [offsets_ref[v, 0] // share for v in range(views)]
    local = [offsets_ref[v, 0] - start[v] * share for v in range(views)]

    def choose(d):
        for j in range(pieces):
            found = jnp.int32(-1)
            for v in range(views):
                found = jnp.where(start[v] + j == d, v, found)
            chosen[d * pieces + j] = found

    each(n_tile, choose)

    current = [states_ref[0, :, r, :] for r in range(height)]
    volume = jnp.concatenate(current, axis=1)
    blocks_copy.wait()
    matrix = fp[...].reshape(views * foot, pixels)
    projected = lax.dot_general(
        volume, matrix, (((1,), (1,)), ((), ())), precision=EXACT,
        preferred_element_type=jnp.float32,
    )
    for v in range(views):
        block = projected[:, v * foot : (v + 1) * foot]
        block = jnp.concatenate([block, jnp.zeros((slices, window - foot), jnp.float32)], axis=1)
        rolled = pltpu.roll(block, local[v], 1)
        for j in range(pieces):
            placed[v, j] = rolled[:, j * share : (j + 1) * share]

    pl.semaphore_wait(
        barrier,
        n_tile - 1 + (n_agent - 1) * (1 + has_low.astype(jnp.int32) + has_high.astype(jnp.int32)),
    )

    def message(d, ref):
        for j in range(pieces):
            v = chosen[d * pieces + j]
            piece = placed[jnp.maximum(v, 0), j]
            ref[d, j * slices : (j + 1) * slices, :] = jnp.where(v >= 0, piece, 0.0)
            ref[d, pieces * slices + j : pieces * slices + j + 1, :] = jnp.full(
                (1, share), v.astype(jnp.float32)
            )

    def forward(d):
        return pltpu.make_async_remote_copy(
            src_ref=fsend.at[d], dst_ref=frecv.at[me], send_sem=fss.at[d], recv_sem=frs.at[me],
            device_id={"tile": d, "agent": ag}, device_id_type=MESH,
        )

    def forward_from(s):
        return pltpu.make_async_remote_copy(
            src_ref=fsend.at[s], dst_ref=frecv.at[s], send_sem=fss.at[s], recv_sem=frs.at[s],
            device_id={"tile": s, "agent": ag}, device_id_type=MESH,
        )

    def send_forward(k):
        d = lax.rem(me + k, n_tile)
        message(d, fsend)
        forward(d).start()

    each(n_tile, send_forward, 1)
    message(me, frecv)

    acc[...] = -measured_ref[...]

    def gather(k):
        s = lax.rem(me + n_tile - k, n_tile)
        if not (isinstance(k, int) and k == 0):
            forward_from(s).wait_recv()
        for j in range(pieces):
            piece = frecv[s, j * slices : (j + 1) * slices, :]
            label = frecv[s, pieces * slices + j : pieces * slices + j + 1, :]
            label = jnp.broadcast_to(label, piece.shape)
            for v in range(views):
                acc[v] += jnp.where(label == v, piece, 0.0)

    gather(0)
    each(n_tile, gather, 1)

    residual = [weights_ref[v] * acc[v] for v in range(views)]

    def answer(s, ref, row):
        for j in range(pieces):
            label = frecv[s, pieces * slices + j : pieces * slices + j + 1, :]
            label = jnp.broadcast_to(label, (slices, share))
            value = jnp.zeros((slices, share), jnp.float32)
            for v in range(views):
                value = jnp.where(label == v, residual[v], value)
            ref[row, j] = value

    def backward(d):
        return pltpu.make_async_remote_copy(
            src_ref=bsend.at[d], dst_ref=brecv.at[me], send_sem=bss.at[d], recv_sem=brs.at[me],
            device_id={"tile": d, "agent": ag}, device_id_type=MESH,
        )

    def backward_from(s):
        return pltpu.make_async_remote_copy(
            src_ref=bsend.at[s], dst_ref=brecv.at[s], send_sem=bss.at[s], recv_sem=brs.at[s],
            device_id={"tile": s, "agent": ag}, device_id_type=MESH,
        )

    def send_backward(k):
        d = lax.rem(me + k, n_tile)
        answer(d, bsend, d)
        backward(d).start()

    each(n_tile, send_backward, 1)
    answer(me, brecv, me)
    each(n_tile, lambda k: backward_from(lax.rem(me + n_tile - k, n_tile)).wait_recv(), 1)

    windows = []
    for v in range(views):
        parts = [brecv[jnp.minimum(start[v] + j, n_tile - 1), j] for j in range(pieces)]
        if window > pieces * share:
            parts.append(jnp.zeros((slices, window - pieces * share), jnp.float32))
        whole = jnp.concatenate(parts, axis=1)
        windows.append(pltpu.roll(whole, window - local[v], 1)[:, :foot])
    gradient = jnp.dot(
        jnp.concatenate(windows, axis=1), matrix, precision=EXACT,
        preferred_element_type=jnp.float32,
    )
    reflect = volume - (2.0 * STEP_SIZE) * gradient
    rsend[...] = reflect

    def share_copy(agent, step):
        return pltpu.make_async_remote_copy(
            src_ref=rsend, dst_ref=rrecv.at[ag, 1 - step],
            send_sem=rss.at[agent, 1 + step], recv_sem=rrs.at[ag, 1 - step],
            device_id={"tile": me + step, "agent": agent}, device_id_type=MESH,
        )

    def share_from(agent, step):
        return pltpu.make_async_remote_copy(
            src_ref=rsend, dst_ref=rrecv.at[agent, 1 + step],
            send_sem=rss.at[agent, 1 + step], recv_sem=rrs.at[agent, 1 + step],
            device_id={"tile": me + step, "agent": agent}, device_id_type=MESH,
        )

    def sharing(act):
        for k in range(1, n_agent):
            act(lax.rem(ag + k, n_agent), 0)
        for step, there in ((-1, has_low), (1, has_high)):

            @pl.when(there)
            def _():
                for k in range(n_agent):
                    act(lax.rem(ag + k, n_agent), step)

    sharing(lambda agent, step: share_copy(agent, step).start())
    rrecv[ag, 1] = reflect

    @pl.when(jnp.logical_not(has_low))
    def _():
        rrecv[:, 0] = jnp.zeros((n_agent, slices, pixels), jnp.float32)

    @pl.when(jnp.logical_not(has_high))
    def _():
        rrecv[:, 2] = jnp.zeros((n_agent, slices, pixels), jnp.float32)

    sharing(lambda agent, step: share_from(agent, step).wait_recv())

    averages = []
    for spot in range(3):
        total = rrecv[0, spot]
        for a in range(1, n_agent):
            total = total + rrecv[a, spot]
        total = total * (1.0 / n_agent)
        averages += [total[:, r * width : (r + 1) * width] for r in range(height)]
    reach = height - SWEEPS
    averages = averages[reach : len(averages) - reach] if reach else averages
    low = jnp.where(has_low, 1.0, 0.0)
    high = jnp.where(has_high, 1.0, 0.0)
    rows, means = averages, averages
    for sweep in range(SWEEPS):
        rows = sweep_rows(rows, means)
        means = means[1:-1]
        outer = SWEEPS - 1 - sweep
        rows = [
            row * low if i < outer else row * high if i >= len(rows) - outer else row
            for i, row in enumerate(rows)
        ]
    for r in range(height):
        mine = reflect[:, r * width : (r + 1) * width]
        prior_ref[:, r, :] = rows[r]
        new_ref[0, :, r, :] = (1.0 - RELAX) * current[r] + RELAX * (2.0 * rows[r] - mine)

    each(n_tile, lambda k: forward(lax.rem(me + k, n_tile)).wait_send(), 1)
    each(n_tile, lambda k: backward(lax.rem(me + k, n_tile)).wait_send(), 1)
    sharing(lambda agent, step: share_copy(agent, step).wait_send())


def shards(n_tile, n_agent, states, footprints, offsets, measured, weights):
    _, slices, height, width = states.shape
    views, _, foot, pixels = footprints.shape
    share = measured.shape[2]
    pieces = (2 * share + foot - 2) // share
    vmem = pl.BlockSpec(memory_space=pltpu.VMEM)
    rows = pieces * slices + pieces
    f32 = jnp.float32
    return tuple(
        pl.pallas_call(
            functools.partial(kernel, n_tile, n_agent),
            out_shape=(
                jax.ShapeDtypeStruct(states.shape, f32),
                jax.ShapeDtypeStruct(states.shape[1:], f32),
            ),
            in_specs=[
                vmem,
                pl.BlockSpec(memory_space=pl.ANY),
                pl.BlockSpec(memory_space=pltpu.SMEM),
                vmem,
                vmem,
            ],
            out_specs=(vmem, vmem),
            scratch_shapes=[
                pltpu.VMEM((views, foot, pixels), f32),
                pltpu.VMEM((views, pieces, slices, share), f32),
                pltpu.SMEM((n_tile * pieces,), jnp.int32),
                pltpu.VMEM((views, slices, share), f32),
                pltpu.VMEM((n_tile, rows, share), f32),
                pltpu.VMEM((n_tile, rows, share), f32),
                pltpu.VMEM((n_tile, pieces, slices, share), f32),
                pltpu.VMEM((n_tile, pieces, slices, share), f32),
                pltpu.VMEM((slices, pixels), f32),
                pltpu.VMEM((n_agent, 3, slices, pixels), f32),
                pltpu.SemaphoreType.DMA,
                pltpu.SemaphoreType.DMA((n_tile,)),
                pltpu.SemaphoreType.DMA((n_tile,)),
                pltpu.SemaphoreType.DMA((n_tile,)),
                pltpu.SemaphoreType.DMA((n_tile,)),
                pltpu.SemaphoreType.DMA((n_agent, 3)),
                pltpu.SemaphoreType.DMA((n_agent, 3)),
            ],
            compiler_params=pltpu.CompilerParams(
                collective_id=0, has_side_effects=True, vmem_limit_bytes=32 * 2**20
            ),
        )(states, footprints, offsets, measured, weights)
    )


def solution(mesh):
    in_specs = (
        P("agent", None, "tile", None),
        P("agent", "tile", None, None),
        P("agent", "tile"),
        P("agent", None, "tile"),
        P("agent", None, "tile"),
    )
    out_specs = (P("agent", None, "tile", None), P(None, "tile", None))
    body = functools.partial(shards, mesh.shape["tile"], mesh.shape["agent"])
    return jax.shard_map(body, mesh=mesh, in_specs=in_specs, out_specs=out_specs, check_vma=False)
```

time: 102 us -> 28.2 us (0.28); the launches traced: 100 us -> 27.9 us
  blocking collectives: 26.4 us -> 0 us
  starting transfers between devices: 23.9 us -> 0 us
  Pallas kernels: 0 us -> 21.8 us
  waiting for transfers between devices: 18.9 us -> 0 us
  between operations: 17.2 us -> 0.64 us
  matrix products: 4.09 us -> 0 us
  other arithmetic: 2.39 us -> 0 us
  local copies, waits for them, and re-layouts: 7.2 us -> 5.4 us
    pallas_call x0 -> x1, Pallas kernels: none -> 21.8 us  [shards(): pl.pallas_call(functools.partial(kernel, n_tile, n_agent), out_shape=(jax...]
    all_to_all x1 -> x0, blocking collectives: 13.9 us -> none  [shards(): lax.all_to_all(outgoing, 'tile', split_axis=0, concat_axis=0, tiled=True)]
    ppermute x8 -> x0, starting transfers between devices: 13 us -> none  [the longest x4 7.85 us: with_halo(): before = lax.ppermute(last, axis, up)]
    ppermute x8 -> x0, waiting for transfers between devices: 12.9 us -> none  [the longest x4 12.9 us: with_halo(): after = lax.ppermute(first, axis, down)]
    all_to_all x2 -> x0, starting transfers between devices: 10.9 us -> none  [the longest x1 7.36 us: shards(): lax.all_to_all(selector, 'tile', split_axis=0, concat_axis=0, tiled=True)]
    unnamed x1 -> x0, blocking collectives: 8.12 us -> none
    all_to_all x2 -> x0, waiting for transfers between devices: 6 us -> none  [the longest x1 6 us: shards(): lax.all_to_all(returned, 'tile', split_axis=0, concat_axis=0, tiled=True)]
    all_gather x1 -> x0, blocking collectives: 4.42 us -> none  [shards(): prior_vol = lax.all_gather(smoothed, 'agent', axis=0, tiled=True)]
  transfers between devices with their start and end apart: 10 -> 0, of which waited for: 5 -> 0; matrix products, arithmetic and copies ran while one was open for 7% -> 0% of each run, Pallas kernels for 0% -> 0%
where the time goes in v1:
time: 28.2 us; the launch traced here: 27.9 us
  Pallas kernels  21.8 us (77%)
  local copies, waits for them, and re-layouts  5.4 us (19%)
  between operations  0.64 us (2%)
    pallas_call x1, Pallas kernels, shards(): pl.pallas_call(functools.partial(kernel, n_tile, n_agent), out_shape=(jax...  21.8 us
    unnamed x11, local copies, waits for them, and re-layouts  5.4 us

profile of v1, /device:TPU:0, one launch (start us, length us, event | category | flops | bytes accessed | tf_op | source)
XLA Modules:
  0.0 27.9 jit_solution(12587063973814164866)
XLA Ops:
  0.6 0.7 %copy.7.offsets_ref = s32[8,1]{1,0:T(8,128)S(1)} copy(s32[8,1]{0,1:T(1,128)} %param.7) | data formatting | bytes 64 | tf_op args[2]
  1.4 0.0 copy-start
  1.4 1.2 %copy-done = f32[8,1,64,512]{3,2,1,0:T(8,128)S(1)} copy-done((f32[8,1,64,512]{3,2,1,0:T(8,128)S(1)}, f32[8,1,64,512]{3,2,1,0:T(8,128)}, u32[]{:S(2)}) %copy-start) | copy-done | bytes 1048600
  2.6 0.0 copy-start.1
  2.6 0.8 %copy-done.1 = f32[8,8,128]{2,1,0:T(8,128)S(1)} copy-done((f32[8,8,128]{2,1,0:T(8,128)S(1)}, f32[8,8,128]{2,1,0:T(8,128)}, u32[]{:S(2)}) %copy-start.1) | copy-done | bytes 32792
  3.3 0.0 copy-start.2
  3.3 0.8 %copy-done.2 = f32[8,8,128]{2,1,0:T(8,128)S(1)} copy-done((f32[8,8,128]{2,1,0:T(8,128)S(1)}, f32[8,8,128]{2,1,0:T(8,128)}, u32[]{:S(2)}) %copy-start.2) | copy-done | bytes 32792
  4.1 0.0 copy-start.3
  4.1 0.7 %copy-done.3 = f32[1,8,2,256]{3,2,1,0:T(2,128)S(1)} copy-done((f32[1,8,2,256]{3,2,1,0:T(2,128)S(1)}, f32[1,8,2,256]{3,2,1,0:T(2,128)}, u32[]{:S(2)}) %copy-start.3) | copy-done | bytes 16408
  4.8 21.8 %shard_map.68 = (f32[1,8,2,256]{3,2,1,0:T(2,128)S(1)}, f32[8,2,256]{2,1,0:T(2,128)S(1)}) custom-call(f32[1,8,2,256]{3,2,1,0:T(2,128)S(1)} %copy-done.3, f32[8,1,64,512]{3,2,1,0:T(8,128)S(1)} %copy-done, s32[8,1]{1,0:T(8,128)S(1)} %copy.7.offsets_ref, f32[8,8,128]{2,1,0:T(8,128)S(1)} %copy-done.1, f32[8,8,128]{2,1,0:T(8,128)S(1)} %copy-done.2), custom_call_target="tpu_custom_call" | custom-call | tf_op jit(solution)/shard_map/pallas_call | solution.py:308
  26.7 0.6 %copy.10 = f32[1,8,2,256]{3,2,1,0:T(2,128)} copy(f32[1,8,2,256]{3,2,1,0:T(2,128)S(1)} %get-tuple-element.4) | data formatting | bytes 32768
  27.3 0.6 %copy.11 = f32[8,2,256]{2,1,0:T(2,128)} copy(f32[8,2,256]{2,1,0:T(2,128)S(1)} %get-tuple-element.5) | data formatting | bytes 32768
Async XLA Ops:
  1.4 1.2 %copy-start = (f32[8,1,64,512]{3,2,1,0:T(8,128)S(1)}, f32[8,1,64,512]{3,2,1,0:T(8,128)}, u32[]{:S(2)}) copy-start(f32[8,1,64,512]{3,2,1,0:T(8,128)} %blocks_hbm.1) | copy-start | bytes 3145732
  2.6 0.8 %copy-start.1 = (f32[8,8,128]{2,1,0:T(8,128)S(1)}, f32[8,8,128]{2,1,0:T(8,128)}, u32[]{:S(2)}) copy-start(f32[8,8,128]{2,1,0:T(8,128)} %measured_ref.1) | copy-start | bytes 98308
  3.3 0.8 %copy-start.2 = (f32[8,8,128]{2,1,0:T(8,128)S(1)}, f32[8,8,128]{2,1,0:T(8,128)}, u32[]{:S(2)}) copy-start(f32[8,8,128]{2,1,0:T(8,128)} %weights_ref.1) | copy-start | bytes 98308
  4.1 0.7 %copy-start.3 = (f32[1,8,2,256]{3,2,1,0:T(2,128)S(1)}, f32[1,8,2,256]{3,2,1,0:T(2,128)}, u32[]{:S(2)}) copy-start(f32[1,8,2,256]{3,2,1,0:T(2,128)} %states_ref.1) | copy-start | bytes 49156

commit v2 on v1

v2 whole, which is shorter than its diff:
```python
import functools

import jax
import jax.numpy as jnp
from jax import lax
from jax.experimental import pallas as pl
from jax.experimental.pallas import tpu as pltpu
from jax.sharding import PartitionSpec as P

SWEEPS = 2
STEP_SIZE = 0.25
RELAX = 0.6
QRATIO = 0.6
MESH = pl.DeviceIdType.MESH


def neighbour_table():
    offsets_nb = []
    for a in (-1, 0, 1):
        for b in (-1, 0, 1):
            for c in (-1, 0, 1):
                if a != 0 or b != 0 or c != 0:
                    offsets_nb.append((a, b, c, a * a + b * b + c * c))
    total = sum(1.0 / item[3] ** 0.5 for item in offsets_nb)
    scale = {n: 4.0 / n**0.5 / total for n in (1, 2, 3)}
    return offsets_nb, scale


def shift_zero(value, step, dim):
    if step == 0:
        return value
    size = value.shape[dim]
    index = lax.broadcasted_iota(jnp.int32, value.shape, dim)
    rolled = pltpu.roll(value, (-step) % size, dim)
    inside = index < size - 1 if step == 1 else index >= 1
    return jnp.where(inside, rolled, 0.0)


def sweep_rows(rows, averages):
    offsets_nb, scale = neighbour_table()
    shifted = [
        {(a, c): shift_zero(shift_zero(row, a, 0), c, 1) for a in (-1, 0, 1) for c in (-1, 0, 1)}
        for row in rows
    ]
    result = []
    for r in range(1, len(rows) - 1):
        centre = rows[r]
        num, den = {}, {}
        for a, b, c, kind in offsets_nb:
            neighbour = shifted[r + b][(a, c)]
            differ = centre - neighbour
            powered = jnp.exp(0.4 * jnp.log(differ * differ))
            inverse = pl.reciprocal(1.0 + powered, approx=True)
            coefficient = inverse * (QRATIO + (1.0 - QRATIO) * inverse)
            num[kind] = num[kind] + coefficient * neighbour if kind in num else coefficient * neighbour
            den[kind] = den[kind] + coefficient if kind in den else coefficient
        top = averages[r] + sum(scale[n] * num[n] for n in num)
        bottom = 1.0 + sum(scale[n] * den[n] for n in den)
        result.append(top / bottom)
    return result


def each(count, body, first=0):
    if count <= 16:
        for k in range(first, count):
            body(k)
    else:
        lax.fori_loop(first, count, lambda k, c: (body(k), c)[1], 0)


def split(value):
    high = value.astype(jnp.bfloat16)
    return high, (value - high.astype(jnp.float32)).astype(jnp.bfloat16)


def lanes(rows, count):
    return lax.broadcasted_iota(jnp.int32, (rows, count), 1)


class Windows:
    def __init__(self, slices, views, foot, share):
        self.slices, self.views, self.foot, self.share = slices, views, foot, share
        self.pieces = (2 * share + foot - 2) // share
        self.width = -(-self.pieces * share // 128) * 128
        self.rows = self.pieces * slices + self.pieces
        self.placed_shape = (self.pieces, slices, share)
        self.back_shape = (self.pieces * slices, share)

    def place(self, block, shift):
        zeros = jnp.zeros((self.slices, self.width - self.foot), jnp.float32)
        rolled = pltpu.roll(jnp.concatenate([block, zeros], axis=1), shift, 1)
        share = self.share
        return jnp.stack([rolled[:, j * share : (j + 1) * share] for j in range(self.pieces)])

    def pack(self, views, shifts, placed):
        parts = [placed[v, j] for j, v in enumerate(views)]
        parts += [jnp.full((1, self.share), v.astype(jnp.float32)) for v in views]
        return jnp.concatenate(parts, axis=0)

    def labels(self, packed):
        base = self.pieces * self.slices
        shape = (self.slices, self.share)
        return [jnp.broadcast_to(packed[base + j : base + j + 1], shape) for j in range(self.pieces)]

    def values(self, packed):
        return [packed[j * self.slices : (j + 1) * self.slices] for j in range(self.pieces)]

    def answer(self, values):
        return jnp.concatenate(values, axis=0)

    def window(self, load, shift):
        parts = [load(j)[j * self.slices : (j + 1) * self.slices] for j in range(self.pieces)]
        rest = self.width - self.pieces * self.share
        if rest:
            parts.append(jnp.zeros((self.slices, rest), jnp.float32))
        whole = jnp.concatenate(parts, axis=1)
        return pltpu.roll(whole, self.width - shift, 1)[:, : self.foot]


class Folded:
    pieces = 2

    def __init__(self, slices, views, foot, share):
        self.slices, self.views, self.foot, self.share = slices, views, foot, share
        self.rows = slices + 2
        self.placed_shape = (1, slices, share)
        self.back_shape = (slices, share)

    def halves(self):
        lane = lanes(self.slices, self.share)
        return lane, lane < self.foot

    def place(self, block, shift):
        lane, lower = self.halves()
        rolled = pltpu.roll(jnp.concatenate([block, block], axis=1), shift, 1)
        spill = shift - self.foot
        slack = jnp.where(lower, spill - 1 - lane, lane - self.foot - spill)
        return jnp.where(slack >= 0, rolled, 0.0)[None]

    def pack(self, views, shifts, placed):
        _, lower = self.halves()
        lane = lanes(1, self.share)
        body = jnp.where(lower, placed[views[1], 0], placed[views[0], 0])
        none = jnp.float32(self.views)
        first = (lane >= shifts[0]) & (lane < shifts[0] + self.foot)
        first = jnp.where(first, views[0].astype(jnp.float32), none)
        second = jnp.where(lane < shifts[1] - self.foot, views[1].astype(jnp.float32), none)
        return jnp.concatenate([body, first, second], axis=0)

    def labels(self, packed):
        shape = (self.slices, self.share)
        base = self.slices
        return [jnp.broadcast_to(packed[base + j : base + j + 1], shape) for j in range(2)]

    def values(self, packed):
        _, lower = self.halves()
        body = packed[: self.slices]
        return [jnp.where(lower, pltpu.roll(body, self.foot, 1), body), body]

    def answer(self, values):
        _, lower = self.halves()
        return jnp.where(lower, values[1], values[0] + pltpu.roll(values[0], self.foot, 1))

    def window(self, load, shift):
        lane, lower = self.halves()
        first, second = load(0), load(1)
        first = jnp.where(lower, pltpu.roll(first, self.foot, 1), first)
        second = jnp.where(lower, second, pltpu.roll(second, self.foot, 1))
        residue = jnp.where(lower, lane, lane - self.foot)
        both = jnp.where(residue < shift - self.foot, second, first)
        return pltpu.roll(both, self.share - shift, 1)[:, : self.foot]


def kernel(
    n_tile, n_agent, form, states_hbm, blocks_hbm, offsets_hbm, measured_hbm, weights_hbm,
    average_ref, base_ref,
    states_ref, fp, offsets_ref, measured_ref, weights_ref,
    fp_high, fp_low, placed, chosen, fsend, frecv, bsend, brecv, rsend, rrecv,
    load_sem, fss, frs, bss, brs, rss, rrs,
):
    me, ag = lax.axis_index("tile"), lax.axis_index("agent")
    slices, height, width = states_ref.shape
    views, foot, pixels = fp.shape
    share = measured_ref.shape[2]
    pieces = form.pieces

    loads = [
        pltpu.make_async_copy(source, target, load_sem.at[i])
        for i, (source, target) in enumerate(
            [
                (offsets_hbm, offsets_ref),
                (states_hbm.at[0], states_ref),
                (blocks_hbm.at[:, 0], fp),
                (measured_hbm, measured_ref),
                (weights_hbm, weights_ref),
            ]
        )
    ]
    for copy in loads:
        copy.start()

    barrier = pltpu.get_barrier_semaphore()

    def greet(tile, agent):
        pl.semaphore_signal(
            barrier, inc=1, device_id={"tile": tile, "agent": agent}, device_id_type=MESH
        )

    each(n_tile, lambda k: greet(lax.rem(me + k, n_tile), ag), 1)
    has_low, has_high = me > 0, me < n_tile - 1
    for k in range(1, n_agent):
        other = lax.rem(ag + k, n_agent)
        greet(me, other)

        @pl.when(has_low)
        def _():
            greet(me - 1, other)

        @pl.when(has_high)
        def _():
            greet(me + 1, other)

    loads[0].wait()
    start = [offsets_ref[0, v] // share for v in range(views)]
    local = [offsets_ref[0, v] - start[v] * share for v in range(views)]

    def choose(d):
        for j in range(pieces):
            found, shift = jnp.int32(views), jnp.int32(0)
            for v in range(views):
                hit = start[v] + j == d
                found = jnp.where(hit, v, found)
                shift = jnp.where(hit, local[v], shift)
            chosen[0, d * pieces + j] = found
            chosen[1, d * pieces + j] = shift

    each(n_tile, choose)
    placed[views] = jnp.zeros(form.placed_shape, jnp.float32)

    loads[1].wait()
    current = [states_ref[:, r, :] for r in range(height)]
    volume = jnp.concatenate(current, axis=1)
    volume_both = jnp.concatenate(split(volume), axis=0)
    loads[2].wait()
    for v in range(views):
        fp_high[v * foot : (v + 1) * foot], fp_low[v * foot : (v + 1) * foot] = split(fp[v])

    def product(left, right):
        return lax.dot_general(
            left, right, (((1,), (1,)), ((), ())), preferred_element_type=jnp.float32
        )

    parts = product(fp_high[...], volume_both)
    extra = product(fp_low[...], volume_both)
    parts = jnp.transpose(parts + jnp.where(lanes(*extra.shape) < slices, extra, 0.0))
    projected = parts[:slices] + parts[slices:]
    for v in range(views):
        placed[v] = form.place(projected[:, v * foot : (v + 1) * foot], local[v])

    pl.semaphore_wait(
        barrier,
        n_tile - 1 + (n_agent - 1) * (1 + has_low.astype(jnp.int32) + has_high.astype(jnp.int32)),
    )

    def message(d):
        spots = [d * pieces + j for j in range(pieces)]
        return form.pack([chosen[0, i] for i in spots], [chosen[1, i] for i in spots], placed)

    def forward(d):
        return pltpu.make_async_remote_copy(
            src_ref=fsend.at[d], dst_ref=frecv.at[me], send_sem=fss.at[d], recv_sem=frs.at[me],
            device_id={"tile": d, "agent": ag}, device_id_type=MESH,
        )

    def forward_from(s):
        return pltpu.make_async_remote_copy(
            src_ref=fsend.at[s], dst_ref=frecv.at[s], send_sem=fss.at[s], recv_sem=frs.at[s],
            device_id={"tile": s, "agent": ag}, device_id_type=MESH,
        )

    def send_forward(k):
        d = lax.rem(me + k, n_tile)
        fsend[d] = message(d)
        forward(d).start()

    each(n_tile, send_forward, 1)
    frecv[me] = message(me)

    loads[3].wait()
    loads[4].wait()

    def add(sums, s):
        packed = frecv[s]
        for label, value in zip(form.labels(packed), form.values(packed)):
            sums = [old + jnp.where(label == v, value, 0.0) for v, old in enumerate(sums)]
        return tuple(sums)

    def gather(k, sums):
        s = lax.rem(me + n_tile - k, n_tile)
        forward_from(s).wait_recv()
        return add(sums, s)

    sums = add([-measured_ref[v] for v in range(views)], me)
    sums = lax.fori_loop(1, n_tile, gather, sums, unroll=n_tile <= 16)
    residual = [weights_ref[v] * sums[v] for v in range(views)]

    def answer(s):
        values = []
        for label in form.labels(frecv[s]):
            value = jnp.zeros((slices, share), jnp.float32)
            for v in range(views):
                value = jnp.where(label == v, residual[v], value)
            values.append(value)
        return form.answer(values)

    def backward(d):
        return pltpu.make_async_remote_copy(
            src_ref=bsend.at[d], dst_ref=brecv.at[me], send_sem=bss.at[d], recv_sem=brs.at[me],
            device_id={"tile": d, "agent": ag}, device_id_type=MESH,
        )

    def backward_from(s):
        return pltpu.make_async_remote_copy(
            src_ref=bsend.at[s], dst_ref=brecv.at[s], send_sem=bss.at[s], recv_sem=brs.at[s],
            device_id={"tile": s, "agent": ag}, device_id_type=MESH,
        )

    def send_backward(k):
        d = lax.rem(me + k, n_tile)
        bsend[d] = answer(d)
        backward(d).start()

    each(n_tile, send_backward, 1)
    brecv[me] = answer(me)
    each(n_tile, lambda k: backward_from(lax.rem(me + n_tile - k, n_tile)).wait_recv(), 1)

    windows = [
        form.window(lambda j: brecv[jnp.minimum(start[v] + j, n_tile - 1)], local[v])
        for v in range(views)
    ]
    high, low = split(jnp.concatenate(windows, axis=1))
    both = jnp.dot(
        jnp.concatenate([high, low], axis=0), fp_high[...], preferred_element_type=jnp.float32
    )
    gradient = both[:slices] + both[slices:]
    gradient += jnp.dot(high, fp_low[...], preferred_element_type=jnp.float32)
    reflect = volume - (2.0 * STEP_SIZE) * gradient
    rsend[...] = reflect

    def share_copy(agent, step):
        return pltpu.make_async_remote_copy(
            src_ref=rsend, dst_ref=rrecv.at[ag, 1 - step],
            send_sem=rss.at[agent, 1 + step], recv_sem=rrs.at[ag, 1 - step],
            device_id={"tile": me + step, "agent": agent}, device_id_type=MESH,
        )

    def share_from(agent, step):
        return pltpu.make_async_remote_copy(
            src_ref=rsend, dst_ref=rrecv.at[agent, 1 + step],
            send_sem=rss.at[agent, 1 + step], recv_sem=rrs.at[agent, 1 + step],
            device_id={"tile": me + step, "agent": agent}, device_id_type=MESH,
        )

    def sharing(act):
        for k in range(1, n_agent):
            act(lax.rem(ag + k, n_agent), 0)
        for step, there in ((-1, has_low), (1, has_high)):

            @pl.when(there)
            def _():
                for k in range(n_agent):
                    act(lax.rem(ag + k, n_agent), step)

    sharing(lambda agent, step: share_copy(agent, step).start())
    rrecv[ag, 1] = reflect

    @pl.when(jnp.logical_not(has_low))
    def _():
        rrecv[:, 0] = jnp.zeros((n_agent, slices, pixels), jnp.float32)

    @pl.when(jnp.logical_not(has_high))
    def _():
        rrecv[:, 2] = jnp.zeros((n_agent, slices, pixels), jnp.float32)

    for r in range(height):
        mine = reflect[:, r * width : (r + 1) * width]
        base_ref[r] = (1.0 - RELAX) * current[r] - RELAX * mine

    each(n_tile, lambda k: forward(lax.rem(me + k, n_tile)).wait_send(), 1)
    each(n_tile, lambda k: backward(lax.rem(me + k, n_tile)).wait_send(), 1)
    sharing(lambda agent, step: share_from(agent, step).wait_recv())

    for spot in range(3):
        total = rrecv[0, spot]
        for a in range(1, n_agent):
            total = total + rrecv[a, spot]
        total = total * (1.0 / n_agent)
        for r in range(height):
            average_ref[spot * height + r] = total[:, r * width : (r + 1) * width]
    sharing(lambda agent, step: share_copy(agent, step).wait_send())


def prior_kernel(n_tile, average_ref, base_ref, new_ref, prior_ref):
    me = lax.axis_index("tile")
    height = base_ref.shape[0]
    reach = height - SWEEPS
    rows = [average_ref[i] for i in range(reach, 3 * height - reach)]
    low = jnp.where(me > 0, 1.0, 0.0)
    high = jnp.where(me < n_tile - 1, 1.0, 0.0)
    means = rows
    for sweep in range(SWEEPS):
        rows = sweep_rows(rows, means)
        means = means[1:-1]
        outer = SWEEPS - 1 - sweep
        rows = [
            row * low if i < outer else row * high if i >= len(rows) - outer else row
            for i, row in enumerate(rows)
        ]
    for r in range(height):
        prior_ref[:, r, :] = rows[r]
        new_ref[0, :, r, :] = base_ref[r] + (2.0 * RELAX) * rows[r]


def shards(n_tile, n_agent, states, footprints, offsets, measured, weights):
    _, slices, height, width = states.shape
    views, _, foot, pixels = footprints.shape
    share = measured.shape[2]
    fold = share == 2 * foot and share % 128 == 0
    form = (Folded if fold else Windows)(slices, views, foot, share)
    vmem = pl.BlockSpec(memory_space=pltpu.VMEM)
    hbm = pl.BlockSpec(memory_space=pltpu.HBM)
    f32 = jnp.float32
    dma = pltpu.SemaphoreType.DMA
    average, base = pl.pallas_call(
        functools.partial(kernel, n_tile, n_agent, form),
        out_shape=(
            jax.ShapeDtypeStruct((3 * height, slices, width), f32),
            jax.ShapeDtypeStruct((height, slices, width), f32),
        ),
        in_specs=[hbm] * 5,
        out_specs=(vmem, vmem),
        scratch_shapes=[
            pltpu.VMEM((slices, height, width), f32),
            pltpu.VMEM((views, foot, pixels), f32),
            pltpu.SMEM((1, views), jnp.int32),
            pltpu.VMEM(measured.shape, f32),
            pltpu.VMEM(weights.shape, f32),
            pltpu.VMEM((views * foot, pixels), jnp.bfloat16),
            pltpu.VMEM((views * foot, pixels), jnp.bfloat16),
            pltpu.VMEM((views + 1,) + form.placed_shape, f32),
            pltpu.SMEM((2, n_tile * form.pieces), jnp.int32),
            pltpu.VMEM((n_tile, form.rows, share), f32),
            pltpu.VMEM((n_tile, form.rows, share), f32),
            pltpu.VMEM((n_tile,) + form.back_shape, f32),
            pltpu.VMEM((n_tile,) + form.back_shape, f32),
            pltpu.VMEM((slices, pixels), f32),
            pltpu.VMEM((n_agent, 3, slices, pixels), f32),
            dma((5,)),
            dma((n_tile,)),
            dma((n_tile,)),
            dma((n_tile,)),
            dma((n_tile,)),
            dma((n_agent, 3)),
            dma((n_agent, 3)),
        ],
        compiler_params=pltpu.CompilerParams(
            collective_id=0, has_side_effects=True, vmem_limit_bytes=60 * 2**20
        ),
    )(states, footprints, offsets.reshape(1, views), measured, weights)
    return tuple(
        pl.pallas_call(
            functools.partial(prior_kernel, n_tile),
            out_shape=(
                jax.ShapeDtypeStruct(states.shape, f32),
                jax.ShapeDtypeStruct(states.shape[1:], f32),
            ),
            in_specs=[vmem, vmem],
            out_specs=(vmem, vmem),
            compiler_params=pltpu.CompilerParams(vmem_limit_bytes=60 * 2**20),
        )(average, base)
    )


def solution(mesh):
    in_specs = (
        P("agent", None, "tile", None),
        P("agent", "tile", None, None),
        P("agent", "tile"),
        P("agent", None, "tile"),
        P("agent", None, "tile"),
    )
    out_specs = (P("agent", None, "tile", None), P(None, "tile", None))
    body = functools.partial(shards, mesh.shape["tile"], mesh.shape["agent"])
    return jax.shard_map(body, mesh=mesh, in_specs=in_specs, out_specs=out_specs, check_vma=False)
```

time: 28.2 us -> 23 us (0.82)
  local copies, waits for them, and re-layouts: 5.4 us -> 0 us
  Pallas kernels: 21.8 us -> 22.1 us
    unnamed x11 -> x0, local copies, waits for them, and re-layouts: 5.4 us -> none
    pallas_call x1 -> x2, Pallas kernels: 21.8 us -> 22.1 us  [the longest x1 20 us: shards(): pl.pallas_call(functools.partial(kernel, n_tile, n_agent, form), out_shap...]
where the time goes in v2:
time: 23 us; the launch traced here: 22.7 us
  Pallas kernels  22.1 us (96%)
  between operations  0.64 us (3%)
    pallas_call x1, Pallas kernels, shards(): pl.pallas_call(functools.partial(kernel, n_tile, n_agent, form), out_shap...  20 us
    pallas_call x1, Pallas kernels, shards(): pl.pallas_call(functools.partial(prior_kernel, n_tile), out_shape=(jax.Sh...  2.11 us

profile of v2, /device:TPU:0, one launch (start us, length us, event | category | flops | bytes accessed | tf_op | source)
XLA Modules:
  0.0 22.7 jit_solution(681050304393348585)
XLA Ops:
  0.6 20.0 %shard_map.68 = (f32[6,8,256]{2,1,0:T(8,128)}, f32[2,8,256]{2,1,0:T(8,128)}) custom-call(f32[1,8,2,256]{3,2,1,0:T(2,128)} %states_hbm.1, f32[8,1,64,512]{3,2,1,0:T(8,128)} %blocks_hbm.1, s32[1,8]{1,0:T(1,128)} %bitcast.1, f32[8,8,128]{2,1,0:T(8,128)} %measured_hbm.1, f32[8,8,128]{2,1,0:T(8,128)} %weights_hbm.1), custom_call_target="tpu_custom_call" | custom-call | tf_op jit(solution)/shard_map/pallas_call | solution.py:434
  20.6 2.1 %shard_map.69 = (f32[1,8,2,256]{3,2,1,0:T(2,128)}, f32[8,2,256]{2,1,0:T(2,128)}) custom-call(f32[6,8,256]{2,1,0:T(8,128)} %get-tuple-element.4.average_ref, f32[2,8,256]{2,1,0:T(8,128)} %get-tuple-element.5.base_ref), custom_call_target="tpu_custom_call" | custom-call | tf_op jit(solution)/shard_map/pallas_call | solution.py:471

commit v3 on v2

--- a/solution.py
+++ b/solution.py
@@ -60,9 +60,13 @@
     return result
 
 
+def far_first(count):
+    return sorted(range(1, count), key=lambda k: -min(k, count - k))
+
+
 def each(count, body, first=0):
     if count <= 16:
-        for k in range(first, count):
+        for k in far_first(count) if first else range(count):
             body(k)
     else:
         lax.fori_loop(first, count, lambda k, c: (body(k), c)[1], 0)
@@ -190,13 +194,13 @@
             [
                 (offsets_hbm, offsets_ref),
                 (states_hbm.at[0], states_ref),
-                (blocks_hbm.at[:, 0], fp),
                 (measured_hbm, measured_ref),
                 (weights_hbm, weights_ref),
             ]
+            + [(blocks_hbm.at[v, 0], fp.at[v]) for v in range(views)]
         )
     ]
-    for copy in loads:
+    for copy in loads[:2] + loads[4:] + loads[2:4]:
         copy.start()
 
     barrier = pltpu.get_barrier_semaphore()
@@ -241,8 +245,8 @@
     current = [states_ref[:, r, :] for r in range(height)]
     volume = jnp.concatenate(current, axis=1)
     volume_both = jnp.concatenate(split(volume), axis=0)
-    loads[2].wait()
     for v in range(views):
+        loads[4 + v].wait()
         fp_high[v * foot : (v + 1) * foot], fp_low[v * foot : (v + 1) * foot] = split(fp[v])
 
     def product(left, right):
@@ -286,8 +290,8 @@
     each(n_tile, send_forward, 1)
     frecv[me] = message(me)
 
+    loads[2].wait()
     loads[3].wait()
-    loads[4].wait()
 
     def add(sums, s):
         packed = frecv[s]
@@ -301,7 +305,11 @@
         return add(sums, s)
 
     sums = add([-measured_ref[v] for v in range(views)], me)
-    sums = lax.fori_loop(1, n_tile, gather, sums, unroll=n_tile <= 16)
+    if n_tile <= 16:
+        for k in reversed(far_first(n_tile)):
+            sums = gather(k, sums)
+    else:
+        sums = lax.fori_loop(1, n_tile, gather, sums)
     residual = [weights_ref[v] * sums[v] for v in range(views)]
 
     def answer(s):
@@ -431,11 +439,13 @@
     hbm = pl.BlockSpec(memory_space=pltpu.HBM)
     f32 = jnp.float32
     dma = pltpu.SemaphoreType.DMA
+    operands = states, footprints, offsets.reshape(1, views), measured, weights
+    operands = [pltpu.with_memory_space_constraint(x, pltpu.HBM) for x in operands]
     average, base = pl.pallas_call(
         functools.partial(kernel, n_tile, n_agent, form),
         out_shape=(
-            jax.ShapeDtypeStruct((3 * height, slices, width), f32),
-            jax.ShapeDtypeStruct((height, slices, width), f32),
+            pltpu.VMEM((3 * height, slices, width), f32),
+            pltpu.VMEM((height, slices, width), f32),
         ),
         in_specs=[hbm] * 5,
         out_specs=(vmem, vmem),
@@ -455,7 +465,7 @@
             pltpu.VMEM((n_tile,) + form.back_shape, f32),
             pltpu.VMEM((slices, pixels), f32),
             pltpu.VMEM((n_agent, 3, slices, pixels), f32),
-            dma((5,)),
+            dma((4 + views,)),
             dma((n_tile,)),
             dma((n_tile,)),
             dma((n_tile,)),
@@ -464,9 +474,9 @@
             dma((n_agent, 3)),
         ],
         compiler_params=pltpu.CompilerParams(
-            collective_id=0, has_side_effects=True, vmem_limit_bytes=60 * 2**20
+            collective_id=0, has_side_effects=True, vmem_limit_bytes=24 * 2**20
         ),
-    )(states, footprints, offsets.reshape(1, views), measured, weights)
+    )(*operands)
     return tuple(
         pl.pallas_call(
             functools.partial(prior_kernel, n_tile),
@@ -476,7 +486,7 @@
             ),
             in_specs=[vmem, vmem],
             out_specs=(vmem, vmem),
-            compiler_params=pltpu.CompilerParams(vmem_limit_bytes=60 * 2**20),
+            compiler_params=pltpu.CompilerParams(vmem_limit_bytes=24 * 2**20),
         )(average, base)
     )
 

time: 23 us -> 23.2 us (level)
  Pallas kernels: 22.1 us -> 22.4 us
    pallas_call x1, Pallas kernels: 20 us -> 21.1 us  [shards(): pl.pallas_call(functools.partial(kernel, n_tile, n_agent, form), out_shap...]
    pallas_call x1, Pallas kernels: 2.11 us -> 1.31 us  [shards(): pl.pallas_call(functools.partial(prior_kernel, n_tile), out_shape=(jax.Sh...]
where the time goes in v3:
time: 23.2 us; the launch traced here: 23 us
  Pallas kernels  22.4 us (97%)
  between operations  0.64 us (3%)
    pallas_call x1, Pallas kernels, shards(): pl.pallas_call(functools.partial(kernel, n_tile, n_agent, form), out_shap...  21.1 us
    pallas_call x1, Pallas kernels, shards(): pl.pallas_call(functools.partial(prior_kernel, n_tile), out_shape=(jax.Sh...  1.31 us

profile of v3, /device:TPU:0, one launch (start us, length us, event | category | flops | bytes accessed | tf_op | source)
XLA Modules:
  0.0 23.0 jit_solution(13125553248011771371)
XLA Ops:
  0.6 21.1 %shard_map.68 = (f32[6,8,256]{2,1,0:T(8,128)S(1)}, f32[2,8,256]{2,1,0:T(8,128)S(1)}) custom-call(f32[1,8,2,256]{3,2,1,0:T(2,128)} %states_hbm.1, f32[8,1,64,512]{3,2,1,0:T(8,128)} %blocks_hbm.1, s32[1,8]{1,0:T(1,128)} %bitcast.1, f32[8,8,128]{2,1,0:T(8,128)} %measured_hbm.1, f32[8,8,128]{2,1,0:T(8,128)} %weights_hbm.1), custom_call_target="tpu_custom_call" | custom-call | tf_op jit(solution)/shard_map/pallas_call | solution.py:444
  21.7 1.3 %shard_map.69 = (f32[1,8,2,256]{3,2,1,0:T(2,128)}, f32[8,2,256]{2,1,0:T(2,128)}) custom-call(f32[6,8,256]{2,1,0:T(8,128)S(1)} %get-tuple-element.4.average_ref, f32[2,8,256]{2,1,0:T(8,128)S(1)} %get-tuple-element.5.base_ref), custom_call_target="tpu_custom_call" | custom-call | tf_op jit(solution)/shard_map/pallas_call | solution.py:481

commit v4 on v3

--- a/solution.py
+++ b/solution.py
@@ -60,13 +60,12 @@
     return result
 
 
-def far_first(count):
-    return sorted(range(1, count), key=lambda k: -min(k, count - k))
+GROUP = 5
 
 
 def each(count, body, first=0):
     if count <= 16:
-        for k in far_first(count) if first else range(count):
+        for k in range(first, count):
             body(k)
     else:
         lax.fori_loop(first, count, lambda k, c: (body(k), c)[1], 0)
@@ -282,12 +281,22 @@
             device_id={"tile": s, "agent": ag}, device_id_type=MESH,
         )
 
-    def send_forward(k):
+    def in_groups(prepare, act):
+        if n_tile > 16:
+            each(n_tile, lambda k: (prepare(k), act(k)), 1)
+            return
+        for low in range(1, n_tile, GROUP):
+            group = range(low, min(low + GROUP, n_tile))
+            for k in group:
+                prepare(k)
+            for k in group:
+                act(k)
+
+    def prepare_forward(k):
         d = lax.rem(me + k, n_tile)
         fsend[d] = message(d)
-        forward(d).start()
-
-    each(n_tile, send_forward, 1)
+
+    in_groups(prepare_forward, lambda k: forward(lax.rem(me + k, n_tile)).start())
     frecv[me] = message(me)
 
     loads[2].wait()
@@ -299,17 +308,18 @@
             sums = [old + jnp.where(label == v, value, 0.0) for v, old in enumerate(sums)]
         return tuple(sums)
 
-    def gather(k, sums):
+    def arrive(k):
         s = lax.rem(me + n_tile - k, n_tile)
         forward_from(s).wait_recv()
-        return add(sums, s)
+        return s
 
     sums = add([-measured_ref[v] for v in range(views)], me)
     if n_tile <= 16:
-        for k in reversed(far_first(n_tile)):
-            sums = gather(k, sums)
+        for low in range(1, n_tile, GROUP):
+            for s in [arrive(k) for k in range(low, min(low + GROUP, n_tile))]:
+                sums = add(sums, s)
     else:
-        sums = lax.fori_loop(1, n_tile, gather, sums)
+        sums = lax.fori_loop(1, n_tile, lambda k, sums: add(sums, arrive(k)), sums)
     residual = [weights_ref[v] * sums[v] for v in range(views)]
 
     def answer(s):
@@ -323,24 +333,24 @@
 
     def backward(d):
         return pltpu.make_async_remote_copy(
-            src_ref=bsend.at[d], dst_ref=brecv.at[me], send_sem=bss.at[d], recv_sem=brs.at[me],
+            src_ref=bsend.at[d], dst_ref=brecv.at[me], send_sem=bss, recv_sem=brs,
             device_id={"tile": d, "agent": ag}, device_id_type=MESH,
         )
 
-    def backward_from(s):
+    def all_backward():
+        count = pl.ds(0, n_tile - 1)
         return pltpu.make_async_remote_copy(
-            src_ref=bsend.at[s], dst_ref=brecv.at[s], send_sem=bss.at[s], recv_sem=brs.at[s],
-            device_id={"tile": s, "agent": ag}, device_id_type=MESH,
-        )
-
-    def send_backward(k):
+            src_ref=bsend.at[count], dst_ref=brecv.at[count], send_sem=bss, recv_sem=brs,
+            device_id={"tile": lax.rem(me + 1, n_tile), "agent": ag}, device_id_type=MESH,
+        )
+
+    def prepare_backward(k):
         d = lax.rem(me + k, n_tile)
         bsend[d] = answer(d)
-        backward(d).start()
-
-    each(n_tile, send_backward, 1)
+
+    in_groups(prepare_backward, lambda k: backward(lax.rem(me + k, n_tile)).start())
     brecv[me] = answer(me)
-    each(n_tile, lambda k: backward_from(lax.rem(me + n_tile - k, n_tile)).wait_recv(), 1)
+    all_backward().wait_recv()
 
     windows = [
         form.window(lambda j: brecv[jnp.minimum(start[v] + j, n_tile - 1)], local[v])
@@ -395,7 +405,7 @@
         base_ref[r] = (1.0 - RELAX) * current[r] - RELAX * mine
 
     each(n_tile, lambda k: forward(lax.rem(me + k, n_tile)).wait_send(), 1)
-    each(n_tile, lambda k: backward(lax.rem(me + k, n_tile)).wait_send(), 1)
+    all_backward().wait_send()
     sharing(lambda agent, step: share_from(agent, step).wait_recv())
 
     for spot in range(3):
@@ -468,8 +478,8 @@
             dma((4 + views,)),
             dma((n_tile,)),
             dma((n_tile,)),
-            dma((n_tile,)),
-            dma((n_tile,)),
+            dma,
+            dma,
             dma((n_agent, 3)),
             dma((n_agent, 3)),
         ],

time: 23.2 us -> 21.1 us (0.909)
  Pallas kernels: 22.4 us -> 20.3 us
    pallas_call x1, Pallas kernels: 21.1 us -> 19 us  [shards(): pl.pallas_call(functools.partial(kernel, n_tile, n_agent, form), out_shap...]
where the time goes in v4:
time: 21.1 us; the launch traced here: 21 us
  Pallas kernels  20.3 us (96%)
  between operations  0.64 us (3%)
    pallas_call x1, Pallas kernels, shards(): pl.pallas_call(functools.partial(kernel, n_tile, n_agent, form), out_shap...  19 us
    pallas_call x1, Pallas kernels, shards(): pl.pallas_call(functools.partial(prior_kernel, n_tile), out_shape=(jax.Sh...  1.31 us

profile of v4, /device:TPU:0, one launch (start us, length us, event | category | flops | bytes accessed | tf_op | source)
XLA Modules:
  0.0 21.0 jit_solution(2183101398574419808)
XLA Ops:
  0.6 19.0 %shard_map.68 = (f32[6,8,256]{2,1,0:T(8,128)S(1)}, f32[2,8,256]{2,1,0:T(8,128)S(1)}) custom-call(f32[1,8,2,256]{3,2,1,0:T(2,128)} %states_hbm.1, f32[8,1,64,512]{3,2,1,0:T(8,128)} %blocks_hbm.1, s32[1,8]{1,0:T(1,128)} %bitcast.1, f32[8,8,128]{2,1,0:T(8,128)} %measured_hbm.1, f32[8,8,128]{2,1,0:T(8,128)} %weights_hbm.1), custom_call_target="tpu_custom_call" | custom-call | tf_op jit(solution)/shard_map/pallas_call | solution.py:454
  19.7 1.3 %shard_map.69 = (f32[1,8,2,256]{3,2,1,0:T(2,128)}, f32[8,2,256]{2,1,0:T(2,128)}) custom-call(f32[6,8,256]{2,1,0:T(8,128)S(1)} %get-tuple-element.4.average_ref, f32[2,8,256]{2,1,0:T(8,128)S(1)} %get-tuple-element.5.base_ref), custom_call_target="tpu_custom_call" | custom-call | tf_op jit(solution)/shard_map/pallas_call | solution.py:491

commit v5 on v4

--- a/solution.py
+++ b/solution.py
@@ -244,26 +244,25 @@
     current = [states_ref[:, r, :] for r in range(height)]
     volume = jnp.concatenate(current, axis=1)
     volume_both = jnp.concatenate(split(volume), axis=0)
-    for v in range(views):
-        loads[4 + v].wait()
-        fp_high[v * foot : (v + 1) * foot], fp_low[v * foot : (v + 1) * foot] = split(fp[v])
-
     def product(left, right):
         return lax.dot_general(
             left, right, (((1,), (1,)), ((), ())), preferred_element_type=jnp.float32
         )
 
-    parts = product(fp_high[...], volume_both)
-    extra = product(fp_low[...], volume_both)
-    parts = jnp.transpose(parts + jnp.where(lanes(*extra.shape) < slices, extra, 0.0))
-    projected = parts[:slices] + parts[slices:]
-    for v in range(views):
-        placed[v] = form.place(projected[:, v * foot : (v + 1) * foot], local[v])
-
-    pl.semaphore_wait(
-        barrier,
-        n_tile - 1 + (n_agent - 1) * (1 + has_low.astype(jnp.int32) + has_high.astype(jnp.int32)),
-    )
+    together = max(1, 128 // foot)
+    for first in range(0, views, together):
+        some = range(first, min(first + together, views))
+        for v in some:
+            loads[4 + v].wait()
+            rows = slice(v * foot, (v + 1) * foot)
+            fp_high[rows], fp_low[rows] = split(fp[v])
+        rows = slice(first * foot, (some[-1] + 1) * foot)
+        parts = product(fp_high[rows], volume_both)
+        extra = product(fp_low[rows], volume_both)
+        parts = jnp.transpose(parts + jnp.where(lanes(*extra.shape) < slices, extra, 0.0))
+        projected = parts[:slices] + parts[slices:]
+        for i, v in enumerate(some):
+            placed[v] = form.place(projected[:, i * foot : (i + 1) * foot], local[v])
 
     def message(d):
         spots = [d * pieces + j for j in range(pieces)]
@@ -296,7 +295,12 @@
         d = lax.rem(me + k, n_tile)
         fsend[d] = message(d)
 
-    in_groups(prepare_forward, lambda k: forward(lax.rem(me + k, n_tile)).start())
+    each(n_tile, prepare_forward, 1)
+    pl.semaphore_wait(
+        barrier,
+        n_tile - 1 + (n_agent - 1) * (1 + has_low.astype(jnp.int32) + has_high.astype(jnp.int32)),
+    )
+    each(n_tile, lambda k: forward(lax.rem(me + k, n_tile)).start(), 1)
     frecv[me] = message(me)
 
     loads[2].wait()

time: 21.1 us -> 21.1 us (level)
  no operation moved by 1% of the time
where the time goes in v5:
time: 21.1 us; the launch traced here: 20.9 us
  Pallas kernels  20.3 us (96%)
  between operations  0.64 us (3%)
    pallas_call x1, Pallas kernels, shards(): pl.pallas_call(functools.partial(kernel, n_tile, n_agent, form), out_shap...  19 us
    pallas_call x1, Pallas kernels, shards(): pl.pallas_call(functools.partial(prior_kernel, n_tile), out_shape=(jax.Sh...  1.31 us

profile of v5, /device:TPU:0, one launch (start us, length us, event | category | flops | bytes accessed | tf_op | source)
XLA Modules:
  0.0 20.9 jit_solution(16036971310557491726)
XLA Ops:
  0.6 19.0 %shard_map.68 = (f32[6,8,256]{2,1,0:T(8,128)S(1)}, f32[2,8,256]{2,1,0:T(8,128)S(1)}) custom-call(f32[1,8,2,256]{3,2,1,0:T(2,128)} %states_hbm.1, f32[8,1,64,512]{3,2,1,0:T(8,128)} %blocks_hbm.1, s32[1,8]{1,0:T(1,128)} %bitcast.1, f32[8,8,128]{2,1,0:T(8,128)} %measured_hbm.1, f32[8,8,128]{2,1,0:T(8,128)} %weights_hbm.1), custom_call_target="tpu_custom_call" | custom-call | tf_op jit(solution)/shard_map/pallas_call | solution.py:458
  19.6 1.3 %shard_map.69 = (f32[1,8,2,256]{3,2,1,0:T(2,128)}, f32[8,2,256]{2,1,0:T(2,128)}) custom-call(f32[6,8,256]{2,1,0:T(8,128)S(1)} %get-tuple-element.4.average_ref, f32[2,8,256]{2,1,0:T(8,128)S(1)} %get-tuple-element.5.base_ref), custom_call_target="tpu_custom_call" | custom-call | tf_op jit(solution)/shard_map/pallas_call | solution.py:495
